TPU v7x, 256 devices: a whole 4x4x8 slice. The times are simulated.
256 devices in a mesh: crop: 32 (over y, z), proto: 8 (over x, core).
Axes of the slice: x: 4, y: 4, z: 8, core: 2. Of those that a mesh axis runs over, the one named last changes fastest.
Arguments:
- student_features: bfloat16 [12288, 256], P('crop'), may hold values from -0.5 to 0.5
- teacher_features: bfloat16 [12288, 256], P('crop'), may hold values from -0.5 to 0.5
- student_weight: bfloat16 [256, 65536], P(None, 'proto'), may hold values from -0.375 to 0.375
- teacher_weight: bfloat16 [256, 65536], P(None, 'proto'), may hold values from -0.5 to 0.5
Outputs:
- weight_grad: float32 [256, 65536], P('crop', 'proto')
- student_gradient: float32 [12288, 256], P('crop', 'proto')
All inputs are finite; a program needn't handle non-finite values.
Results may differ from a plain program's by a relative error of at most 0.0058.
The roundings to bfloat16 on the way count: a program that leaves them out, or rounds other values in their place, can miss the bound.
Values sent between devices are 32-bit elements; how exact they have to be, the bound alone decides.
A program may use at most 128 MiB of HBM per device.

v0:
```python
import jax
import jax.numpy as jnp
from jax import lax
from jax.sharding import PartitionSpec as P

BALANCE_STEPS = 3
LOSS_SCALE = 4194304


EPSILON = 1e-06
TEACHER_TEMP = 0.07
STUDENT_TEMP = 0.1


def unit_rows(features):
    wide = features.astype(jnp.float32)
    row_norms = jnp.sqrt(jnp.sum(wide * wide, axis=1, keepdims=True) + EPSILON)
    return (wide / row_norms, row_norms)


def unit_columns(weight):
    wide = weight.astype(jnp.float32)
    column_norm_values = jnp.sqrt(jnp.sum(wide * wide, axis=0) + EPSILON)
    return (wide / column_norm_values, column_norm_values)


def shards(student_features, teacher_features, student_weight, teacher_weight):
    row_count = student_features.shape[0]
    feat_width = student_features.shape[1]
    crops_all = row_count * lax.axis_size("crop")
    t_unit, t_norms = unit_rows(teacher_features)
    t_bf = t_unit.astype(jnp.bfloat16)
    s_unit, s_norms = unit_rows(student_features)
    s_bf = s_unit.astype(jnp.bfloat16)
    tw_unit, tw_norms = unit_columns(teacher_weight)
    tw_bf = tw_unit.astype(jnp.bfloat16)
    sw_unit, sw_norms = unit_columns(student_weight)
    sw_bf = sw_unit.astype(jnp.bfloat16)
    teacher_exp = jnp.exp(jnp.dot(t_bf, tw_bf, preferred_element_type=jnp.float32) / TEACHER_TEMP)
    row_scale = jnp.ones((row_count,), jnp.float32)
    col_scale = jnp.ones((teacher_exp.shape[1],), jnp.float32)
    for balance_iteration in range(BALANCE_STEPS):
        col_sums = lax.psum(jnp.sum(teacher_exp * row_scale[:, None], axis=0), "crop")
        col_scale = 1.0 / col_sums
        row_sums = lax.psum(jnp.sum(teacher_exp * col_scale[None, :], axis=1), "proto")
        row_scale = 1.0 / row_sums
    cosine = jnp.dot(s_bf, sw_bf, preferred_element_type=jnp.float32)
    student_exp = jnp.exp(cosine / STUDENT_TEMP)
    row_total = lax.psum(jnp.sum(student_exp, axis=1), "proto")
    targets = teacher_exp * row_scale[:, None] * col_scale[None, :]
    student_prob = student_exp / row_total[:, None]
    factor = LOSS_SCALE / (STUDENT_TEMP * crops_all)
    logit_grad = ((student_prob - targets) * factor).astype(jnp.bfloat16)
    d_piece = feat_width // lax.axis_size("crop")
    grad_share = lax.psum_scatter(
        lax.dot_general(
            s_bf, logit_grad, (((0,), (0,)), ((), ())), preferred_element_type=jnp.float32
        ),
        "crop",
        scatter_dimension=0,
        tiled=True,
    )
    d_offset = lax.axis_index("crop") * d_piece
    unit_share = lax.dynamic_slice_in_dim(sw_unit, d_offset, d_piece, 0)
    bf_share = lax.dynamic_slice_in_dim(sw_bf, d_offset, d_piece, 0)
    proto_inner = lax.psum(jnp.sum(bf_share.astype(jnp.float32) * grad_share, axis=0), "crop")
    weight_grad = (grad_share - unit_share * proto_inner[None, :]) / sw_norms[None, :]
    feat_terms = lax.dot_general(
        logit_grad, sw_bf, (((1,), (1,)), ((), ())), preferred_element_type=jnp.float32
    )
    c_piece = feat_width // lax.axis_size("proto")
    col_offset = lax.axis_index("proto") * c_piece
    feat_grad = lax.psum(feat_terms, "proto")
    crop_inner = jnp.sum(s_bf.astype(jnp.float32) * feat_grad, axis=1)
    whole_grad = (feat_grad - s_unit * crop_inner[:, None]) / s_norms
    student_gradient = lax.dynamic_slice_in_dim(whole_grad, col_offset, c_piece, 1)
    return (weight_grad, student_gradient)


def solution(mesh):
    return jax.shard_map(
        shards,
        mesh=mesh,
        in_specs=(P("crop", None), P("crop", None), P(None, "proto"), P(None, "proto")),
        out_specs=(P("crop", "proto"), P("crop", "proto")),
        check_vma=False,
    )
```

profile of v0, /device:TPU:4, one launch (start us, length us, event | category | flops | bytes accessed | tf_op | source)
XLA Modules:
  0.0 915.9 jit_solution(17414106876954594155)
XLA Ops:
  8.0 0.0 all-reduce.3.cloned.1.call-start
  8.0 3.1 fusion.1
  11.1 1.1 fusion.6
  12.2 9.9 %fusion.15 = (f32[8192]{0:T(1024)S(1)}, f32[384,8192]{1,0:T(8,128)}) fusion(bf16[256,8192]{1,0:T(8,128)(2,1)} %param.7, f32[8192]{0:T(1024)S(1)} %add_sqrt_fusion, bf16[384,256]{1,0:T(8,128)(2,1)} %param.5, f32[384]{0:T(512)S(1)} %add_sqrt_fusion.2), kind=kOutput, calls=%fused_computation.44 | convolution fusion | flops 1623482368 | bytes 17040896 | tf_op jit(solution)/shard_map/dot_general | solution.py:39
  22.1 145.9 %psum.64 = f32[8192]{0:T(1024)S(1)} all-reduce(f32[8192]{0:T(1024)S(1)} %get-tuple-element.10), channel_id=1, replica_groups=mesh['crop'=32,'proto'=8] {'crop'}, use_global_device_ids=true, to_apply=%region_7.0 | all-reduce | flops 8192 | bytes 65536 | tf_op jit(solution)/shard_map/psum | solution.py:43
  168.1 5.7 multiply_reduce_fusion.4
  173.8 10.2 %psum.65 = f32[384]{0:T(512)S(1)} all-reduce(f32[384]{0:T(512)S(1)} %multiply_reduce_fusion.4), channel_id=1, replica_groups=mesh['crop'=32,'proto'=8] {'proto'}, use_global_device_ids=true, to_apply=%region_9.0 | all-reduce | flops 384 | bytes 3072 | tf_op jit(solution)/shard_map/psum | solution.py:45
  184.1 6.3 multiply_reduce_fusion.3
  190.4 137.7 %psum.66 = f32[8192]{0:T(1024)S(1)} all-reduce(f32[8192]{0:T(1024)S(1)} %multiply_reduce_fusion.3), channel_id=1, replica_groups=mesh['crop'=32,'proto'=8] {'crop'}, use_global_device_ids=true, to_apply=%region_11.0 | all-reduce | flops 8192 | bytes 65536 | tf_op jit(solution)/shard_map/psum | solution.py:43
  328.1 5.7 multiply_reduce_fusion.2
  333.8 10.0 %psum.67 = f32[384]{0:T(512)S(1)} all-reduce(f32[384]{0:T(512)S(1)} %multiply_reduce_fusion.2), channel_id=1, replica_groups=mesh['crop'=32,'proto'=8] {'proto'}, use_global_device_ids=true, to_apply=%region_13.0 | all-reduce | flops 384 | bytes 3072 | tf_op jit(solution)/shard_map/psum | solution.py:45
  343.8 6.3 multiply_reduce_fusion.1
  350.1 137.8 %psum.68 = f32[8192]{0:T(1024)S(1)} all-reduce(f32[8192]{0:T(1024)S(1)} %multiply_reduce_fusion.1), channel_id=1, replica_groups=mesh['crop'=32,'proto'=8] {'crop'}, use_global_device_ids=true, to_apply=%region_15.0 | all-reduce | flops 8192 | bytes 65536 | tf_op jit(solution)/shard_map/psum | solution.py:43
  487.9 0.0 copy-start.3
  488.0 5.9 multiply_reduce_fusion
  493.8 0.0 copy-done.3
  493.8 0.9 fusion
  494.7 0.0 copy-start.4
  494.8 4.6 convert_divide_fusion.1
  499.4 0.0 copy-done.4
  499.4 0.0 copy-start.1
  499.4 0.1 fusion.5
  499.5 5.7 fusion.16
  505.2 0.0 copy-done.1
  505.2 11.3 %all-reduce = (f32[384]{0:T(512)S(1)}, f32[384]{0:T(512)S(1)}) all-reduce(f32[384]{0:T(512)S(1)} %multiply_reduce_fusion, f32[384]{0:T(512)S(1)} %get-tuple-element.12), channel_id=1, replica_groups=mesh['crop'=32,'proto'=8] {'proto'}, use_global_device_ids=true, to_apply=%region_17.0 | all-reduce | flops 768 | bytes 6144 | tf_op jit(solution)/shard_map/psum | solution.py:45
  516.5 0.0 copy-start.2
  516.5 9.6 %multiply_convert_fusion = bf16[384,8192]{1,0:T(8,128)(2,1)S(1)} fusion(f32[384,8192]{1,0:T(8,128)} %get-tuple-element.11, f32[384,8192]{1,0:T(8,128)} %get-tuple-element.13, f32[384]{0:T(512)S(1)} %broadcast_divide_fusion.3, f32[8192]{0:T(1024)S(1)} %broadcast_divide_fusion, f32[384]{0:T(512)S(1)} %get-tuple-element.5), kind=kLoop, calls=%fused_computation | loop fusion | flops 18874368 | bytes 31493120 | tf_op jit(solution)/shard_map/convert_element_type | solution.py:53
  526.2 0.0 copy-start
  526.2 2.7 copy-done
  528.9 0.0 copy-done.2
  528.9 2.6 fusion.17
  531.5 0.0 all-reduce.3.cloned.1.call-update
  531.5 0.0 reduce-scatter.2.cloned.1.call-start
  531.5 8.5 fusion.11
  540.0 0.0 reduce-scatter.2.cloned.1.call-update
  540.0 51.0 %all-reduce.3.cloned.1.call-done = f32[384,256]{1,0:T(8,128)} async-done(((f32[384,256]{1,0:T(8,128)}), f32[384,256]{1,0:T(8,128)}) %all-reduce.3.cloned.1.call-update) | async-done | bytes 393232 | tf_op jit(solution)/shard_map/psum | solution.py:73
  591.0 1.2 multiply_reduce_fusion.5
  592.2 1.2 fusion.9
  593.4 0.7 copy.6
  594.2 170.9 %reduce-scatter.2.cloned.1.call-done = f32[8,8192]{1,0:T(8,128)} async-done(((f32[256,8192]{1,0:T(8,128)}), f32[8,8192]{1,0:T(8,128)}) %reduce-scatter.2.cloned.1.call-update) | async-done | bytes 262160 | tf_op jit(solution)/shard_map/reduce_scatter | solution.py:55
  765.1 1.1 multiply_reduce_fusion.6
  766.2 140.4 %psum.70 = f32[8192]{0:T(1024)S(1)} all-reduce(f32[8192]{0:T(1024)S(1)} %multiply_reduce_fusion.6), channel_id=1, replica_groups=mesh['crop'=32,'proto'=8] {'crop'}, use_global_device_ids=true, to_apply=%region_20.0 | all-reduce | flops 8192 | bytes 65536 | tf_op jit(solution)/shard_map/psum | solution.py:66
  906.6 1.8 subtract_divide_fusion
  (10 shorter events, 0.1 us)
Async XLA Ops:
  8.0 583.0 %all-reduce.3.cloned.1.call-start = ((), (), s32[]{:S(2)}) async-start(), calls=%async_computation.2 | async-start | bytes 786432 | tf_op jit(solution)/shard_map/psum | solution.py:73
  487.9 5.9 copy-start.3
  494.7 4.6 copy-start.4
  499.4 5.8 copy-start.1
  516.5 12.4 %copy-start.2 = (bf16[256,8192]{1,0:T(8,128)(2,1)S(1)}, bf16[256,8192]{1,0:T(8,128)(2,1)}, u32[]{:S(2)}) copy-start(bf16[256,8192]{1,0:T(8,128)(2,1)} %copy-done.1) | copy-start | bytes 12582916
  526.2 2.7 copy-start
  531.5 233.6 %reduce-scatter.2.cloned.1.call-start = ((), (), s32[]{:S(2)}) async-start(), calls=%async_computation.1 | async-start | bytes 8650752 | tf_op jit(solution)/shard_map/reduce_scatter | solution.py:55
Sparse Core Ops, SparseCore 0:
  531.6 59.3 all-reduce.2
Sparse Core Ops, SparseCore 1:
  540.1 224.9 reduce-scatter.1
where the time goes:
time: 916 us
  blocking collectives  593 us (65%)
  waiting for transfers between devices  222 us (24%)
  other arithmetic  54.7 us (6%)
  matrix products  26.7 us (3%)
  between operations  15.6 us (2%)
    psum x3, blocking collectives, shards(): lax.psum(jnp.sum(teacher_exp * row_scale[:, None], axis=0), 'crop')  421 us
    reduce_scatter x1, waiting for transfers between devices, shards(): lax.psum_scatter(lax.dot_general(s_bf, logit_grad, (((0,), (0,)), ((), ()...  171 us
    psum x1, blocking collectives, shards(): lax.psum(jnp.sum(bf_share.astype(jnp.float32) * grad_share, axis=0), 'crop')  140 us
    psum x1, waiting for transfers between devices, shards(): feat_grad = lax.psum(feat_terms, 'proto')  51 us
    psum x3, blocking collectives, shards(): lax.psum(jnp.sum(teacher_exp * col_scale[None, :], axis=1), 'proto')  31.5 us
  transfers between devices with their start and end apart: 2, of which 2 were waited for; matrix products, arithmetic and copies ran while one was open for 1% of the time, Pallas kernels for 0%

commit v1 on v0

v1 whole, which is shorter than its diff:
```python
import functools
import math

import jax
import jax.numpy as jnp
from jax import lax
from jax.experimental import pallas as pl
from jax.experimental.pallas import tpu as pltpu
from jax.sharding import PartitionSpec as P

BALANCE_STEPS = 3
LOSS_SCALE = 4194304
EPSILON = 1e-06
TEACHER_TEMP = 0.07
STUDENT_TEMP = 0.1
LOG2E = math.log2(math.e)

NY, NZ, NX, NC = 4, 8, 4, 2
D = 256
ROWS = 384
TILE_ROWS = NY * ROWS
TILE_COLS = 2048
HALF = TILE_COLS // 2
QUARTER = TILE_COLS // 4
BLOCKS = TILE_ROWS // 128
MESH = pl.DeviceIdType.MESH
F32, BF16 = jnp.float32, jnp.bfloat16


def kernel(
    factor,
    t_ref, s_ref, tw_hbm, sw_hbm,
    wout_ref, hout_ref,
    E, A, tw_raw, sw_raw, tw_bf, sw_bf, sw_t, sw_inv, t_bf, s_bf, s_t, s_unit, s_inv,
    u_wide, z_wide, t_src, s_src, t_in, s_in,
    c_src, c_in, r_src, r_in, z_src, z_in, v_ref,
    L, G, ring_r, ring_l, g_sum, g_out, H, HT, h_core, h_in,
    load_sem, t_send, t_recv, t_fsend, t_frecv, s_send, s_recv, s_fsend, s_frecv,
    c_send, c_recv, r_send, r_recv, z_send, z_recv,
    rr_send, rr_recv, rl_send, rl_recv, a_send, a_recv, hc_send, hc_recv, h_send, h_recv,
):
    crop, proto = lax.axis_index("crop"), lax.axis_index("proto")
    y, z, x, c = crop // NZ, crop % NZ, proto // NC, proto % NC

    def dev(dy, dz, dx, dc):
        return (((y + dy) % NY) * NZ + (z + dz) % NZ, ((x + dx) % NX) * NC + (c + dc) % NC)

    def remote(src, dst, send, recv, to):
        return pltpu.make_async_remote_copy(
            src_ref=src, dst_ref=dst, send_sem=send, recv_sem=recv, device_id=to, device_id_type=MESH
        )

    def wait_bytes(buf, sem):
        pltpu.make_async_copy(buf, buf, sem).wait()

    plane = [
        (dy, dx, dc) for dy in range(NY) for dx in range(NX) for dc in range(NC) if (dy, dx, dc) != (0, 0, 0)
    ]
    sheet = [(dy, dx) for dy in range(NY) for dx in range(NX) if (dy, dx) != (0, 0)]

    barrier = pltpu.get_barrier_semaphore()
    for dy, dx, dc in plane:
        pl.semaphore_signal(barrier, inc=1, device_id=dev(dy, 0, dx, dc), device_id_type=MESH)
    for dz in range(1, NZ):
        pl.semaphore_signal(barrier, inc=1, device_id=dev(0, dz, 0, 0), device_id_type=MESH)

    col0 = pl.multiple_of(y * TILE_COLS, TILE_COLS)
    load_t = pltpu.make_async_copy(tw_hbm.at[:, pl.ds(col0, TILE_COLS)], tw_raw, load_sem.at[0])
    load_s = pltpu.make_async_copy(sw_hbm.at[:, pl.ds(col0, TILE_COLS)], sw_raw, load_sem.at[1])
    load_t.start()
    load_s.start()

    def block_rows(block):
        return pl.ds(pl.multiple_of(block * ROWS, ROWS), ROWS)

    t32 = t_ref[...].astype(F32)
    t_own = (t32 * (1.0 / jnp.sqrt(jnp.sum(t32 * t32, axis=1, keepdims=True) + EPSILON))).astype(BF16)
    t_bf[block_rows(y), :] = t_own
    t_src[...] = t_own.astype(F32).reshape(2, ROWS // 2, D)
    s_src[...] = s_ref[...].astype(F32).reshape(2, ROWS // 2, D)

    pl.semaphore_wait(barrier, len(plane) + NZ - 1)

    def gather_start(src, dst, send, recv):
        for o in (1, 3, 2):
            remote(src.at[c], dst.at[o - 1, c], send, recv.at[o - 1], dev(o, 0, 0, 0)).start()

    def gather_forward(dst, recv, fsend, frecv, o):
        wait_bytes(dst.at[o - 1, c], recv.at[o - 1])
        remote(dst.at[o - 1, c], dst.at[o - 1, c], fsend, frecv.at[o - 1], dev(0, 0, 0, 1)).start()

    gather_start(t_src, t_in, t_send, t_recv)

    load_t.wait()

    def normalise(q, carry, raw, out, inv_ref):
        cols = pl.ds(pl.multiple_of(q * QUARTER, QUARTER), QUARTER)
        w = raw[:, cols].astype(F32)
        inv = 1.0 / jnp.sqrt(jnp.sum(w * w, axis=0, keepdims=True) + EPSILON)
        out[:, cols] = (w * inv).astype(BF16)
        if inv_ref is not None:
            inv_ref[:, cols] = inv
        return carry

    lax.fori_loop(0, 4, functools.partial(normalise, raw=tw_raw, out=tw_bf, inv_ref=None), 0)

    def exp_block(block, first):
        rows = block_rows(block)

        def one(q, carry):
            cols = pl.ds(pl.multiple_of(q * QUARTER, QUARTER), QUARTER)
            e = jnp.exp2(
                jnp.dot(t_bf[rows, :], tw_bf[:, cols], preferred_element_type=F32) * (LOG2E / TEACHER_TEMP)
            )
            E[rows, cols] = e
            part = jnp.sum(e.reshape(ROWS // 8, 8, QUARTER), axis=0)
            c_acc = part if first else part + v_ref[:, cols]
            v_ref[:, cols] = c_acc
            return carry

        lax.fori_loop(0, 4, one, 0)

    exp_block(y, True)
    load_s.wait()
    lax.fori_loop(0, 4, functools.partial(normalise, raw=sw_raw, out=sw_bf, inv_ref=sw_inv), 0)
    for o in (1, 3, 2):
        gather_forward(t_in, t_recv, t_fsend, t_frecv, o)
    gather_start(s_src, s_in, s_send, s_recv)
    for o in (1, 3, 2):
        wait_bytes(t_in.at[o - 1, 1 - c], t_frecv.at[o - 1])
        block = (y + NY - o) % NY
        t_bf[block_rows(block), :] = t_in[o - 1].reshape(ROWS, D).astype(BF16)
        exp_block(block, False)

    def cols_start(r, sums):
        c_src[r] = jnp.sum(sums, axis=0, keepdims=True)
        for dz in range(1, NZ):
            remote(c_src.at[r], c_in.at[r, dz - 1], c_send.at[r], c_recv.at[r], dev(0, dz, 0, 0)).start()

    def cols_done(r):
        wait_bytes(c_in.at[r], c_recv.at[r])
        total = c_src[r]
        for dz in range(1, NZ):
            total = total + c_in[r, dz - 1]
        return 1.0 / total

    def rows_of(src, dst, scale):
        def one(b, carry):
            rows = pl.ds(pl.multiple_of(b * 128, 128), 128)
            acc = None
            for k in range(TILE_COLS // 128):
                term = src[rows, k * 128:(k + 1) * 128]
                if scale is not None:
                    term = term * scale[:, k * 128:(k + 1) * 128]
                acc = term if acc is None else acc + term
            dst[pl.ds(b, 1), :] = jnp.sum(acc.T, axis=0, keepdims=True)
            return carry

        lax.fori_loop(0, BLOCKS, one, 0)

    def rows_start(src, dst, send, recv):
        for i, (dy, dx, dc) in enumerate(plane):
            remote(src, dst.at[i], send, recv, dev(dy, 0, dx, dc)).start()

    def rows_done(src, dst, recv):
        wait_bytes(dst, recv)
        total = src[...]
        for i in range(len(plane)):
            total = total + dst[i]
        return 1.0 / total

    def widen(dst, flat):
        for b in range(BLOCKS):
            dst[b * 128:(b + 1) * 128, :] = jnp.broadcast_to(flat[b:b + 1, :], (128, 128)).T

    def cols_of():
        def one(b, acc):
            rows = pl.ds(pl.multiple_of(b * 128, 128), 128)
            u = u_wide[rows, :]
            out = []
            for k in range(TILE_COLS // 128):
                e = E[rows, k * 128:(k + 1) * 128] * u
                out.append(acc[k] + jnp.sum(e.reshape(16, 8, 128), axis=0))
            return tuple(out)

        zero = tuple(jnp.zeros((8, 128), F32) for _ in range(TILE_COLS // 128))
        acc = lax.fori_loop(0, BLOCKS, one, zero)
        return jnp.concatenate(acc, axis=1)

    def student_exp(b0, b1):
        def one(i, carry):
            b, q = i // 4, i % 4
            rows = pl.ds(pl.multiple_of(b * ROWS, ROWS), ROWS)
            cols = pl.ds(pl.multiple_of(q * QUARTER, QUARTER), QUARTER)
            A[rows, cols] = jnp.exp2(
                jnp.dot(s_bf[rows, :], sw_bf[:, cols], preferred_element_type=F32) * (LOG2E / STUDENT_TEMP)
            )
            return carry

        lax.fori_loop(b0 * 4, b1 * 4, one, 0)

    def student_block(block, raw):
        inv = 1.0 / jnp.sqrt(jnp.sum(raw * raw, axis=1, keepdims=True) + EPSILON)
        unit = raw * inv
        rows = block_rows(block)
        s_unit[rows, :] = unit
        s_inv[rows, :] = jnp.broadcast_to(inv, (ROWS, 128))
        s_bf[rows, :] = unit.astype(BF16)

    cols_start(0, v_ref[...])
    student_block(y, s_src[...].reshape(ROWS, D))
    for q in range(4):
        sw_t[q * QUARTER:(q + 1) * QUARTER, :] = sw_bf[:, q * QUARTER:(q + 1) * QUARTER].T
    v = cols_done(0)
    rows_of(E, r_src.at[0], v)
    rows_start(r_src.at[0], r_in.at[0], r_send.at[0], r_recv.at[0])
    for o in (1, 3, 2):
        gather_forward(s_in, s_recv, s_fsend, s_frecv, o)
    widen(u_wide, rows_done(r_src.at[0], r_in.at[0], r_recv.at[0]))
    cols_start(1, cols_of())
    for o in (1, 3, 2):
        wait_bytes(s_in.at[o - 1, 1 - c], s_frecv.at[o - 1])
        student_block((y + NY - o) % NY, s_in[o - 1].reshape(ROWS, D))
    v = cols_done(1)
    rows_of(E, r_src.at[1], v)
    rows_start(r_src.at[1], r_in.at[1], r_send.at[1], r_recv.at[1])
    student_exp(0, 3)
    widen(u_wide, rows_done(r_src.at[1], r_in.at[1], r_recv.at[1]))
    cols_start(2, cols_of())
    student_exp(3, 4)
    rows_of(A, z_src, None)
    v = cols_done(2)
    v_ref[0:1, :] = v
    rows_of(E, r_src.at[2], v)
    rows_start(r_src.at[2], r_in.at[2], r_send.at[2], r_recv.at[2])
    rows_start(z_src, z_in, z_send, z_recv)
    for b in range(BLOCKS):
        s_t[:, b * 128:(b + 1) * 128] = s_bf[b * 128:(b + 1) * 128, :].T
    widen(z_wide, rows_done(z_src, z_in, z_recv) * factor)
    widen(u_wide, rows_done(r_src.at[2], r_in.at[2], r_recv.at[2]) * factor)

    def quarter(q):
        lo = q * QUARTER

        def one(b, carry):
            rows = pl.ds(pl.multiple_of(b * 128, 128), 128)
            u, w = u_wide[rows, :], z_wide[rows, :]
            for k in range(QUARTER // 128):
                at = slice(lo + k * 128, lo + (k + 1) * 128)
                grad = A[rows, at] * w - E[rows, at] * u * v_ref[0:1, at]
                L[rows, k * 128:(k + 1) * 128] = grad.astype(BF16)
            return carry

        lax.fori_loop(0, BLOCKS, one, 0)
        cols = slice(lo, lo + QUARTER)
        g = jnp.dot(s_t[...], L[...], preferred_element_type=F32)
        inv = sw_inv[:, cols]
        inner = jnp.sum(sw_bf[:, cols].astype(F32) * g, axis=0, keepdims=True)
        g = (g - sw_raw[:, cols].astype(F32) * (inv * inner)) * inv
        at = (q % 2) * QUARTER
        G[q // 2, :, :, :, at:at + QUARTER] = g.reshape(NY, NZ, 8, QUARTER)
        def rows_h(b, carry):
            rows = pl.ds(pl.multiple_of(b * ROWS, ROWS), ROWS)
            h = jnp.dot(L[rows, :], sw_t[cols, :], preferred_element_type=F32)
            H[rows, :] = h if q == 0 else H[rows, :] + h
            return carry

        lax.fori_loop(0, NY, rows_h, 0)

    def ring(i, buf, send, recv, way):
        half = i % 2 if way == 1 else 1 - i % 2
        hops = NZ // 2 - (i + 1) // 2
        dest = (z + way * hops + NZ) % NZ
        if i < 2:
            src = G.at[half, :, dest]
        else:
            wait_bytes(buf.at[i - 2], recv.at[i - 2])
            buf[i - 2] = buf[i - 2] + G[half, :, dest]
            src = buf.at[i - 2]
        remote(src, buf.at[i], send.at[i], recv.at[i], dev(0, way, 0, 0)).start()

    def ring_right(i):
        ring(i, ring_r, rr_send, rr_recv, 1)

    def ring_left(i):
        ring(i, ring_l, rl_send, rl_recv, -1)

    quarter(0)
    quarter(1)
    ring_right(0)
    quarter(2)
    quarter(3)
    ring_left(0)
    ring_right(1)
    ring_left(1)

    def finish_h(b, carry):
        rows = pl.ds(pl.multiple_of(b * 128, 128), 128)
        h = H[rows, :]
        inner = jnp.sum(s_bf[rows, :].astype(F32) * h, axis=1, keepdims=True)
        inv = s_inv[rows, :]
        h = (h - s_unit[rows, :] * inner) * jnp.concatenate([inv, inv], axis=1)
        turned = h.T
        for p in range(NX * NC):
            HT[p % NC, p // NC, :, rows] = turned[p * 32:(p + 1) * 32, :]
        return carry

    lax.fori_loop(0, BLOCKS, finish_h, 0)
    core = remote(HT.at[1 - c], h_core, hc_send, hc_recv, dev(0, 0, 0, 1))
    core.start()
    ring_right(2)
    ring_left(2)
    core.wait_recv()

    def add_h(i, carry):
        HT[c, i] = HT[c, i] + h_core[i]
        return carry

    lax.fori_loop(0, NX, add_h, 0)
    for i, (dy, dx) in enumerate(sheet):
        to_y, to_x = (y + dy) % NY, (x + dx) % NX
        remote(
            HT.at[c, to_x, :, block_rows(to_y)], h_in.at[i], h_send, h_recv, dev(dy, 0, dx, 0)
        ).start()
    for i in range(3, 7):
        ring_right(i)
        ring_left(i)

    wait_bytes(h_in, h_recv)
    total = HT[c, x, :, block_rows(y)]
    for i in range(len(sheet)):
        total = total + h_in[i]
    hout_ref[...] = total

    def turn(half, last_r, last_l):
        wait_bytes(ring_r.at[last_r], rr_recv.at[last_r])
        wait_bytes(ring_l.at[last_l], rl_recv.at[last_l])
        g_sum[half] = G[half, :, z] + ring_r[last_r] + ring_l[last_l]
        for o in range(1, NY):
            remote(
                g_sum.at[half, (y + o) % NY], g_out.at[half, o - 1], a_send.at[half], a_recv.at[half], dev(o, 0, 0, 0)
            ).start()
        wout_ref[:, pl.ds(pl.multiple_of(y * TILE_COLS + half * HALF, HALF), HALF)] = g_sum[half, y]

    turn(0, 6, 5)
    turn(1, 5, 6)
    for half in range(2):
        wait_bytes(g_out.at[half], a_recv.at[half])
        for o in range(1, NY):
            at = pl.multiple_of(((y + NY - o) % NY) * TILE_COLS + half * HALF, HALF)
            wout_ref[:, pl.ds(at, HALF)] = g_out[half, o - 1]

    wait_bytes(t_in.at[:, 0], t_send)
    wait_bytes(t_in.at[:, 0], t_fsend)
    wait_bytes(s_in.at[:, 0], s_send)
    wait_bytes(s_in.at[:, 0], s_fsend)
    for r in range(BALANCE_STEPS):
        wait_bytes(c_in.at[r], c_send.at[r])
        wait_bytes(r_in.at[r], r_send.at[r])
    wait_bytes(z_in, z_send)
    for i in range(7):
        wait_bytes(ring_r.at[i], rr_send.at[i])
        wait_bytes(ring_l.at[i], rl_send.at[i])
    core.wait_send()
    wait_bytes(h_in, h_send)
    for half in range(2):
        wait_bytes(g_out.at[half], a_send.at[half])


def shards(student_features, teacher_features, student_weight, teacher_weight):
    crops_all = student_features.shape[0] * lax.axis_size("crop")
    factor = LOSS_SCALE / (STUDENT_TEMP * crops_all)
    vmem = pl.BlockSpec(memory_space=pltpu.VMEM)
    hbm = pl.BlockSpec(memory_space=pl.ANY)
    peers, sheet = NY * NX * NC - 1, NY * NX - 1
    v = pltpu.VMEM
    dma = pltpu.SemaphoreType.DMA
    scratch = [
        v((TILE_ROWS, TILE_COLS), F32), v((TILE_ROWS, TILE_COLS), F32),
        v((D, TILE_COLS), BF16), v((D, TILE_COLS), BF16),
        v((D, TILE_COLS), BF16), v((D, TILE_COLS), BF16),
        v((TILE_COLS, D), BF16), v((1, TILE_COLS), F32),
        v((TILE_ROWS, D), BF16), v((TILE_ROWS, D), BF16), v((D, TILE_ROWS), BF16),
        v((TILE_ROWS, D), F32), v((TILE_ROWS, 128), F32),
        v((TILE_ROWS, 128), F32), v((TILE_ROWS, 128), F32),
        v((2, ROWS // 2, D), F32), v((2, ROWS // 2, D), F32),
        v((NY - 1, 2, ROWS // 2, D), F32), v((NY - 1, 2, ROWS // 2, D), F32),
        v((BALANCE_STEPS, 1, TILE_COLS), F32), v((BALANCE_STEPS, NZ - 1, 1, TILE_COLS), F32),
        v((BALANCE_STEPS, BLOCKS, 128), F32), v((BALANCE_STEPS, peers, BLOCKS, 128), F32),
        v((BLOCKS, 128), F32), v((peers, BLOCKS, 128), F32),
        v((8, TILE_COLS), F32),
        v((TILE_ROWS, QUARTER), BF16),
        v((2, NY, NZ, 8, HALF), F32),
        v((7, NY, 8, HALF), F32), v((7, NY, 8, HALF), F32),
        v((2, NY, 8, HALF), F32), v((2, NY - 1, 8, HALF), F32),
        v((TILE_ROWS, D), F32), v((NC, NX, 32, TILE_ROWS), F32),
        v((NX, 32, TILE_ROWS), F32), v((sheet, 32, ROWS), F32),
        dma((2,)),
        dma, dma((3,)), dma, dma((3,)),
        dma, dma((3,)), dma, dma((3,)),
        dma((3,)), dma((3,)), dma((3,)), dma((3,)), dma, dma,
        dma((7,)), dma((7,)), dma((7,)), dma((7,)),
        dma((2,)), dma((2,)), dma, dma, dma, dma,
    ]
    weight_grad, turned = pl.pallas_call(
        functools.partial(kernel, factor),
        out_shape=(
            jax.ShapeDtypeStruct((D // (NY * NZ), NY * TILE_COLS), F32),
            jax.ShapeDtypeStruct((D // (NX * NC), ROWS), F32),
        ),
        in_specs=[vmem, vmem, hbm, hbm],
        out_specs=(vmem, vmem),
        scratch_shapes=scratch,
        compiler_params=pltpu.CompilerParams(
            collective_id=0, has_side_effects=True, vmem_limit_bytes=60 * 1024 * 1024
        ),
        name="prototype_head",
    )(teacher_features, student_features, teacher_weight, student_weight)
    return weight_grad, turned.T


def solution(mesh):
    return jax.shard_map(
        shards,
        mesh=mesh,
        in_specs=(P("crop", None), P("crop", None), P(None, "proto"), P(None, "proto")),
        out_specs=(P("crop", "proto"), P("crop", "proto")),
        check_vma=False,
    )
```

time: 916 us -> 107 us (0.12)
  the two profiles are of different devices: /device:TPU:4 before, /device:TPU:1 now
where the time goes in v1:
time: 107 us
  Pallas kernels  103 us (96%)
  local copies, waits for them, and re-layouts  3.09 us (3%)
    pallas_call x1, Pallas kernels, shards(): pl.pallas_call(functools.partial(kernel, factor), out_shape=(jax.ShapeDty...  103 us
    unnamed x2, local copies, waits for them, and re-layouts  3.09 us

profile of v1, /device:TPU:1, one launch (start us, length us, event | category | flops | bytes accessed | tf_op | source)
XLA Modules:
  0.0 107.1 jit_solution(8547250253059021517)
XLA Ops:
  0.6 103.3 %prototype_head.1 = (f32[8,8192]{1,0:T(8,128)}, f32[32,384]{1,0:T(8,128)}) custom-call(bf16[384,256]{1,0:T(8,128)(2,1)} %t_ref.1, bf16[384,256]{1,0:T(8,128)(2,1)} %s_ref.1, bf16[256,8192]{1,0:T(8,128)(2,1)} %tw_hbm.1, bf16[256,8192]{1,0:T(8,128)(2,1)} %sw_hbm.1), custom_call_target="tpu_custom_call" | custom-call | tf_op jit(solution)/shard_map/prototype_head/pallas_call | solution.py:405
  104.0 1.7 %copy.8 = f32[8,8192]{1,0:T(8,128)} copy(f32[8,8192]{1,0:T(8,128)} %get-tuple-element.8) | data formatting | bytes 524288
  105.7 1.4 %copy.9 = f32[384,32]{0,1:T(8,128)} copy(f32[384,32]{0,1:T(8,128)} %bitcast.1) | data formatting | bytes 98304

commit v2 on v1

v2 whole, which is shorter than its diff:
```python
import functools
import math

import jax
import jax.numpy as jnp
from jax import lax
from jax.experimental import pallas as pl
from jax.experimental.pallas import tpu as pltpu
from jax.sharding import PartitionSpec as P

BALANCE_STEPS = 3
LOSS_SCALE = 4194304
EPSILON = 1e-06
TEACHER_TEMP = 0.07
STUDENT_TEMP = 0.1
LOG2E = math.log2(math.e)

NY, NZ, NX, NC = 4, 8, 4, 2
D = 256
ROWS = 384
TILE_ROWS = NY * ROWS
TILE_COLS = 2048
HALF = TILE_COLS // 2
QUARTER = TILE_COLS // 4
BLOCKS = TILE_ROWS // 128
PIECE = ROWS // 4
MESH = pl.DeviceIdType.MESH
F32, BF16 = jnp.float32, jnp.bfloat16


def kernel(
    factor,
    t_ref, s_ref, tw_hbm, sw_hbm,
    wout_ref, hout_ref,
    E, A, tw_raw, sw_raw, tw_bf, sw_bf, sw_t, sw_inv, t_bf, s_bf, s_t, s_raw, s_inv,
    u_wide, part, t_src, s_src, t_in, s_in,
    c_src, c_in, r_src, r_in, flat_ref, v_ref,
    L, G, ring_r, ring_l, g_sum, g_out, h_core, h_in,
    load_sem, t_send, t_recv, t_fsend, t_frecv, s_send, s_recv, s_fsend, s_frecv,
    c_send, c_recv, r_send, r_recv,
    rr_send, rr_recv, rl_send, rl_recv, a_send, a_recv, hc_send, hc_recv, h_send, h_recv,
):
    crop, proto = lax.axis_index("crop"), lax.axis_index("proto")
    y, z, x, c = crop // NZ, crop % NZ, proto // NC, proto % NC

    def dev(dy, dz, dx, dc):
        return (((y + dy) % NY) * NZ + (z + dz) % NZ, ((x + dx) % NX) * NC + (c + dc) % NC)

    def remote(src, dst, send, recv, to):
        return pltpu.make_async_remote_copy(
            src_ref=src, dst_ref=dst, send_sem=send, recv_sem=recv, device_id=to, device_id_type=MESH
        )

    def wait_bytes(buf, sem):
        pltpu.make_async_copy(buf, buf, sem).wait()

    def far(d, n):
        return min(d, n - d)

    plane = sorted(
        ((dy, dx, dc) for dy in range(NY) for dx in range(NX) for dc in range(NC) if (dy, dx, dc) != (0, 0, 0)),
        key=lambda o: -(far(o[0], NY) + far(o[1], NX)),
    )
    sheet = sorted(
        ((dy, dx) for dy in range(NY) for dx in range(NX) if (dy, dx) != (0, 0)),
        key=lambda o: -(far(o[0], NY) + far(o[1], NX)),
    )
    line = sorted(range(1, NZ), key=lambda d: -far(d, NZ))

    barrier = pltpu.get_barrier_semaphore()
    for dy, dx, dc in plane:
        pl.semaphore_signal(barrier, inc=1, device_id=dev(dy, 0, dx, dc), device_id_type=MESH)
    for dz in line:
        pl.semaphore_signal(barrier, inc=1, device_id=dev(0, dz, 0, 0), device_id_type=MESH)

    col0 = pl.multiple_of(y * TILE_COLS, TILE_COLS)
    load_t = pltpu.make_async_copy(tw_hbm.at[:, pl.ds(col0, TILE_COLS)], tw_raw, load_sem.at[0])
    load_s = pltpu.make_async_copy(sw_hbm.at[:, pl.ds(col0, TILE_COLS)], sw_raw, load_sem.at[1])
    load_t.start()
    load_s.start()

    def block_rows(block):
        return pl.ds(pl.multiple_of(block * ROWS, ROWS), ROWS)

    def normalise(raw, out, inv_ref):
        def one(q, carry):
            cols = pl.ds(pl.multiple_of(q * QUARTER, QUARTER), QUARTER)
            w = raw[:, cols].astype(F32)
            inv = 1.0 / jnp.sqrt(jnp.sum(w * w, axis=0, keepdims=True) + EPSILON)
            out[:, cols] = (w * inv).astype(BF16)
            if inv_ref is not None:
                inv_ref[:, cols] = inv
            return carry

        lax.fori_loop(0, 4, one, 0)

    t32 = t_ref[...].astype(F32)
    t_own = (t32 * (1.0 / jnp.sqrt(jnp.sum(t32 * t32, axis=1, keepdims=True) + EPSILON))).astype(BF16)
    t_bf[block_rows(y), :] = t_own
    t_src[...] = t_own.astype(F32).reshape(2, 2, PIECE, D)
    s_src[...] = s_ref[...].astype(F32).reshape(2, 2, PIECE, D)

    pl.semaphore_wait(barrier, len(plane) + NZ - 1)

    def gather_start(src, dst, send, recv):
        for piece, way in ((0, 1), (1, 3), (1, 1), (0, 3)):
            remote(src.at[c, piece], dst.at[way - 1, c, piece], send, recv.at[way - 1, piece], dev(way, 0, 0, 0)).start()

    def gather_relay(dst, send, recv):
        for piece, way in ((0, 1), (1, 3)):
            wait_bytes(dst.at[way - 1, c, piece], recv.at[way - 1, piece])
            remote(
                dst.at[way - 1, c, piece], dst.at[1, c, piece], send, recv.at[1, piece], dev(way, 0, 0, 0)
            ).start()

    def gather_core(dst, fsend, frecv, way, piece):
        remote(
            dst.at[way - 1, c, piece], dst.at[way - 1, c, piece], fsend, frecv.at[way - 1, piece], dev(0, 0, 0, 1)
        ).start()

    def gather_near(dst, recv, fsend, frecv):
        gather_core(dst, fsend, frecv, 1, 0)
        gather_core(dst, fsend, frecv, 3, 1)
        for piece, way in ((1, 1), (0, 3)):
            wait_bytes(dst.at[way - 1, c, piece], recv.at[way - 1, piece])
            gather_core(dst, fsend, frecv, way, piece)

    def gather_far(dst, recv, fsend, frecv):
        for piece in range(2):
            wait_bytes(dst.at[1, c, piece], recv.at[1, piece])
            gather_core(dst, fsend, frecv, 2, piece)

    def gather_done(dst, frecv, way):
        for piece in range(2):
            wait_bytes(dst.at[way - 1, 1 - c, piece], frecv.at[way - 1, piece])
        return (y + NY - way) % NY, dst[way - 1].reshape(ROWS, D)

    gather_start(t_src, t_in, t_send, t_recv)
    load_t.wait()
    normalise(tw_raw, tw_bf, None)

    def exp_block(block, first):
        rows = block_rows(block)

        def one(q, carry):
            cols = pl.ds(pl.multiple_of(q * HALF, HALF), HALF)
            e = jnp.exp2(
                jnp.dot(t_bf[rows, :], tw_bf[:, cols], preferred_element_type=F32) * (LOG2E / TEACHER_TEMP)
            )
            E[rows, cols] = e
            sums = jnp.sum(e.reshape(ROWS // 8, 8, HALF), axis=0)
            v_ref[:, cols] = sums if first else sums + v_ref[:, cols]
            return carry

        lax.fori_loop(0, 2, one, 0)

    exp_block(y, True)
    gather_relay(t_in, t_send, t_recv)
    load_s.wait()
    normalise(sw_raw, sw_bf, sw_inv)
    gather_near(t_in, t_recv, t_fsend, t_frecv)
    for way in (1, 3, 2):
        if way == 3:
            gather_far(t_in, t_recv, t_fsend, t_frecv)
        block, rows = gather_done(t_in, t_frecv, way)
        t_bf[block_rows(block), :] = rows.astype(BF16)
        exp_block(block, False)

    def cols_start(r, sums):
        c_src[r] = jnp.sum(sums, axis=0, keepdims=True)
        for i, dz in enumerate(line):
            remote(c_src.at[r], c_in.at[r, i], c_send.at[r], c_recv.at[r], dev(0, dz, 0, 0)).start()

    def cols_done(r):
        wait_bytes(c_in.at[r], c_recv.at[r])
        total = c_src[r]
        for i in range(len(line)):
            total = total + c_in[r, i]
        return 1.0 / total

    lane = lax.broadcasted_iota(jnp.int32, (8, 128), 1)
    sublane = lax.broadcasted_iota(jnp.int32, (8, 128), 0)

    def rows_of(src, r, scale, store):
        def one(b, carry):
            rows = pl.ds(pl.multiple_of(b * 128, 128), 128)
            acc = None
            for k in range(TILE_COLS // 128):
                cols = slice(k * 128, (k + 1) * 128)
                term = src[rows, cols]
                if scale is not None:
                    term = term * scale[:, cols]
                if store:
                    src[rows, cols] = term
                acc = term if acc is None else acc + term
            part[rows, :] = acc
            return carry

        lax.fori_loop(0, BLOCKS, one, 0)

        def packed(g0, g1):
            out = None
            for base in range(g0, g1, 16):
                some = jnp.zeros((8, 128), F32)
                for g in range(base, base + 16):
                    total = jnp.sum(part[8 * g:8 * g + 8, :], axis=1, keepdims=True)
                    some = jnp.where(lane == g - g0, total, some)
                out = some if out is None else out + some
            return out

        r_src[r, 0:8, :] = packed(0, 128)
        rest = packed(128, 192)
        rest = rest + pltpu.roll(pltpu.roll(rest, 64, 1), 4, 0)
        r_src[r, 8:12, :] = rest[0:4, :]

    def rows_start(r):
        for i, (dy, dx, dc) in enumerate(plane):
            remote(r_src.at[r], r_in.at[r, i], r_send.at[r], r_recv.at[r], dev(dy, 0, dx, dc)).start()

    def rows_done(r, dst, scale):
        wait_bytes(r_in.at[r], r_recv.at[r])
        total = r_src[r]
        for i in range(len(plane)):
            total = total + r_in[r, i]
        flat_ref[0:BLOCKS, :] = scale / total
        low, rest = flat_ref[0:8, :], flat_ref[8:16, :]
        high = jnp.where(sublane < 4, rest, pltpu.roll(pltpu.roll(rest, 64, 1), 4, 0))
        for g in range(TILE_ROWS // 8):
            value = low[:, g:g + 1] if g < 128 else high[:, g - 128:g - 127]
            dst[8 * g:8 * g + 8, :] = jnp.broadcast_to(value, (8, 128))

    def cols_of():
        def one(b, acc):
            rows = pl.ds(pl.multiple_of(b * 128, 128), 128)
            u = u_wide[rows, :]
            out = []
            for k in range(TILE_COLS // 128):
                e = E[rows, k * 128:(k + 1) * 128] * u
                out.append(acc[k] + jnp.sum(e.reshape(16, 8, 128), axis=0))
            return tuple(out)

        zero = tuple(jnp.zeros((8, 128), F32) for _ in range(TILE_COLS // 128))
        acc = lax.fori_loop(0, BLOCKS, one, zero)
        return jnp.concatenate(acc, axis=1)

    def student_exp():
        def one(i, carry):
            rows = pl.ds(pl.multiple_of((i // 2) * ROWS, ROWS), ROWS)
            cols = pl.ds(pl.multiple_of((i % 2) * HALF, HALF), HALF)
            A[rows, cols] = jnp.exp2(
                jnp.dot(s_bf[rows, :], sw_bf[:, cols], preferred_element_type=F32) * (LOG2E / STUDENT_TEMP)
            )
            return carry

        lax.fori_loop(0, 2 * NY, one, 0)

    def student_block(block, raw):
        inv = 1.0 / jnp.sqrt(jnp.sum(raw * raw, axis=1, keepdims=True) + EPSILON)
        unit = raw * inv
        rows = block_rows(block)
        s_raw[rows, :] = raw.astype(BF16)
        s_inv[rows, :] = jnp.broadcast_to(inv, (ROWS, 128))
        s_bf[rows, :] = unit.astype(BF16)

    cols_start(0, v_ref[...])
    gather_start(s_src, s_in, s_send, s_recv)
    student_block(y, s_src[...].reshape(ROWS, D))
    for q in range(4):
        sw_t[q * QUARTER:(q + 1) * QUARTER, :] = sw_bf[:, q * QUARTER:(q + 1) * QUARTER].T
    v = cols_done(0)
    rows_of(E, 0, v, False)
    rows_start(0)
    gather_relay(s_in, s_send, s_recv)
    gather_near(s_in, s_recv, s_fsend, s_frecv)
    rows_done(0, u_wide, 1.0)
    cols_start(1, cols_of())
    gather_far(s_in, s_recv, s_fsend, s_frecv)
    for way in (1, 3, 2):
        student_block(*gather_done(s_in, s_frecv, way))
    v = cols_done(1)
    rows_of(E, 1, v, False)
    rows_start(1)
    student_exp()
    rows_done(1, u_wide, 1.0)
    cols_start(2, cols_of())
    rows_of(A, 3, None, False)
    rows_start(3)
    v = cols_done(2)
    rows_of(E, 2, v, True)
    rows_start(2)
    for b in range(BLOCKS):
        s_t[:, b * 128:(b + 1) * 128] = s_bf[b * 128:(b + 1) * 128, :].T
    z_wide = part
    rows_done(3, z_wide, factor)

    def probs(b, carry):
        rows = pl.ds(pl.multiple_of(b * 128, 128), 128)
        w = z_wide[rows, :]
        for k in range(TILE_COLS // 128):
            A[rows, k * 128:(k + 1) * 128] = A[rows, k * 128:(k + 1) * 128] * w
        return carry

    lax.fori_loop(0, BLOCKS, probs, 0)
    rows_done(2, u_wide, factor)

    def quarter(q):
        lo = q * QUARTER

        def one(b, carry):
            rows = pl.ds(pl.multiple_of(b * 128, 128), 128)
            u = u_wide[rows, :]
            for k in range(QUARTER // 128):
                at = slice(lo + k * 128, lo + (k + 1) * 128)
                L[rows, at] = (A[rows, at] - E[rows, at] * u).astype(BF16)
            return carry

        lax.fori_loop(0, BLOCKS, one, 0)
        cols = slice(lo, lo + QUARTER)
        g = jnp.dot(s_t[...], L[:, cols], preferred_element_type=F32)
        inv = sw_inv[:, cols]
        inner = jnp.sum(sw_bf[:, cols].astype(F32) * g, axis=0, keepdims=True)
        g = (g - sw_raw[:, cols].astype(F32) * (inv * inner)) * inv
        G[q] = g.reshape(NY, NZ, 8, QUARTER)

    def steps(q, way):
        return NZ // 2 if (q < 2) == (way == 1) else NZ // 2 - 1

    def ring(q, k, way):
        buf, send, recv = (ring_r, rr_send, rr_recv) if way == 1 else (ring_l, rl_send, rl_recv)
        if k >= steps(q, way):
            return
        dest = (z + way * (steps(q, way) - k) + NZ) % NZ
        if k == 0:
            src = G.at[q, :, dest]
        else:
            wait_bytes(buf.at[q, k - 1], recv.at[q, k - 1])
            buf[q, k - 1] = buf[q, k - 1] + G[q, :, dest]
            src = buf.at[q, k - 1]
        remote(src, buf.at[q, k], send.at[q, k], recv.at[q, k], dev(0, way, 0, 0)).start()

    def turned_rows(core_of, x_of, count):
        return pl.ds(pl.multiple_of((core_of * NX + x_of) * 32, 32), 32 * count)

    def h_block(b):
        rows = slice(b * ROWS, (b + 1) * ROWS)
        A[rows, 0:D] = jnp.dot(L[rows, :], sw_t[...], preferred_element_type=F32)

    def h_finish():
        def one(b, carry):
            rows = pl.ds(pl.multiple_of(b * 128, 128), 128)
            h = A[rows, 0:D]
            inner = jnp.sum(s_bf[rows, :].astype(F32) * h, axis=1, keepdims=True)
            inv = jnp.concatenate([s_inv[rows, :]] * 2, axis=1)
            h = (h - s_raw[rows, :].astype(F32) * inv * inner) * inv
            turned = h.T
            for p in range(NX * NC):
                E[turned_rows(p % NC, p // NC, 1), rows] = turned[p * 32:(p + 1) * 32, :]
            return carry

        lax.fori_loop(0, BLOCKS, one, 0)

    core = remote(E.at[turned_rows(1 - c, 0, NX), 0:TILE_ROWS], h_core, hc_send, hc_recv, dev(0, 0, 0, 1))

    def h_spread():
        core.wait_recv()

        def add(i, carry):
            here = turned_rows(c, i, 1)
            E[here, 0:TILE_ROWS] = E[here, 0:TILE_ROWS] + h_core[pl.ds(pl.multiple_of(i * 32, 32), 32), :]
            return carry

        lax.fori_loop(0, NX, add, 0)
        for i, (dy, dx) in enumerate(sheet):
            to_y, to_x = (y + dy) % NY, (x + dx) % NX
            remote(
                E.at[turned_rows(c, to_x, 1), block_rows(to_y)], h_in.at[i], h_send, h_recv, dev(dy, 0, dx, 0)
            ).start()

    def h_done():
        wait_bytes(h_in, h_recv)
        total = E[turned_rows(c, x, 1), block_rows(y)]
        for i in range(len(sheet)):
            total = total + h_in[i]
        hout_ref[...] = total

    between = [
        lambda: (h_block(0), h_block(1)), lambda: (h_block(2), h_block(3)), lambda: (h_finish(), core.start()),
        lambda: None, h_spread,
    ]

    for q in range(4):
        quarter(q)
        ring(q, 0, 1)
        ring(q, 0, -1)
    for k in range(1, NZ // 2):
        for q in range(4):
            ring(q, k, 1)
            ring(q, k, -1)
            if between:
                between.pop(0)()

    for q in range(4):
        last_r, last_l = steps(q, 1) - 1, steps(q, -1) - 1
        wait_bytes(ring_r.at[q, last_r], rr_recv.at[q, last_r])
        wait_bytes(ring_l.at[q, last_l], rl_recv.at[q, last_l])
        g_sum[q] = G[q, :, z] + ring_r[q, last_r] + ring_l[q, last_l]
        for o in (2, 1, 3):
            remote(
                g_sum.at[q, (y + o) % NY], g_out.at[q, o - 1], a_send.at[q], a_recv.at[q], dev(o, 0, 0, 0)
            ).start()
        wout_ref[:, pl.ds(pl.multiple_of(y * TILE_COLS + q * QUARTER, QUARTER), QUARTER)] = g_sum[q, y]
    h_done()
    for q in range(4):
        wait_bytes(g_out.at[q], a_recv.at[q])
        for o in range(1, NY):
            at = pl.multiple_of(((y + NY - o) % NY) * TILE_COLS + q * QUARTER, QUARTER)
            wout_ref[:, pl.ds(at, QUARTER)] = g_out[q, o - 1]

    for buf, send, fsend in ((t_in, t_send, t_fsend), (s_in, s_send, s_fsend)):
        wait_bytes(buf.at[:, 0], send)
        wait_bytes(buf.at[:, 0], fsend)
    for r in range(BALANCE_STEPS):
        wait_bytes(c_in.at[r], c_send.at[r])
    for r in range(BALANCE_STEPS + 1):
        wait_bytes(r_in.at[r], r_send.at[r])
    for q in range(4):
        for k in range(steps(q, 1)):
            wait_bytes(ring_r.at[q, k], rr_send.at[q, k])
        for k in range(steps(q, -1)):
            wait_bytes(ring_l.at[q, k], rl_send.at[q, k])
        wait_bytes(g_out.at[q], a_send.at[q])
    core.wait_send()
    wait_bytes(h_in, h_send)


def shards(student_features, teacher_features, student_weight, teacher_weight):
    crops_all = student_features.shape[0] * lax.axis_size("crop")
    factor = LOSS_SCALE / (STUDENT_TEMP * crops_all)
    vmem = pl.BlockSpec(memory_space=pltpu.VMEM)
    hbm = pl.BlockSpec(memory_space=pl.ANY)
    peers, sheet = NY * NX * NC - 1, NY * NX - 1
    v = pltpu.VMEM
    dma = pltpu.SemaphoreType.DMA
    scratch = [
        v((TILE_ROWS, TILE_COLS), F32), v((TILE_ROWS, TILE_COLS), F32),
        v((D, TILE_COLS), BF16), v((D, TILE_COLS), BF16),
        v((D, TILE_COLS), BF16), v((D, TILE_COLS), BF16),
        v((TILE_COLS, D), BF16), v((1, TILE_COLS), F32),
        v((TILE_ROWS, D), BF16), v((TILE_ROWS, D), BF16), v((D, TILE_ROWS), BF16),
        v((TILE_ROWS, D), BF16), v((TILE_ROWS, 128), F32),
        v((TILE_ROWS, 128), F32), v((TILE_ROWS, 128), F32),
        v((2, 2, PIECE, D), F32), v((2, 2, PIECE, D), F32),
        v((NY - 1, 2, 2, PIECE, D), F32), v((NY - 1, 2, 2, PIECE, D), F32),
        v((BALANCE_STEPS, 1, TILE_COLS), F32), v((BALANCE_STEPS, NZ - 1, 1, TILE_COLS), F32),
        v((BALANCE_STEPS + 1, BLOCKS, 128), F32), v((BALANCE_STEPS + 1, peers, BLOCKS, 128), F32),
        v((16, 128), F32), v((8, TILE_COLS), F32),
        v((TILE_ROWS, TILE_COLS), BF16),
        v((4, NY, NZ, 8, QUARTER), F32),
        v((4, NZ // 2, NY, 8, QUARTER), F32), v((4, NZ // 2, NY, 8, QUARTER), F32),
        v((4, NY, 8, QUARTER), F32), v((4, NY - 1, 8, QUARTER), F32),
        v((NX * 32, TILE_ROWS), F32), v((sheet, 32, ROWS), F32),
        dma((2,)),
        dma, dma((3, 2)), dma, dma((3, 2)),
        dma, dma((3, 2)), dma, dma((3, 2)),
        dma((3,)), dma((3,)), dma((4,)), dma((4,)),
        dma((4, 4)), dma((4, 4)), dma((4, 4)), dma((4, 4)),
        dma((4,)), dma((4,)), dma, dma, dma, dma,
    ]
    weight_grad, turned = pl.pallas_call(
        functools.partial(kernel, factor),
        out_shape=(
            jax.ShapeDtypeStruct((D // (NY * NZ), NY * TILE_COLS), F32),
            jax.ShapeDtypeStruct((D // (NX * NC), ROWS), F32),
        ),
        in_specs=[vmem, vmem, hbm, hbm],
        out_specs=(vmem, vmem),
        scratch_shapes=scratch,
        compiler_params=pltpu.CompilerParams(
            collective_id=0, has_side_effects=True, vmem_limit_bytes=53 * 1024 * 1024
        ),
        name="prototype_head",
    )(teacher_features, student_features, teacher_weight, student_weight)
    def hand_over(a_ref, b_ref, a_out, b_out):
        a_out[...] = a_ref[...]
        b_out[...] = b_ref[...]

    weight_grad, turned = pl.pallas_call(
        hand_over,
        out_shape=(
            jax.ShapeDtypeStruct(weight_grad.shape, F32),
            jax.ShapeDtypeStruct(turned.shape, F32),
        ),
        in_specs=[vmem, vmem],
        out_specs=(vmem, vmem),
        name="hand_over",
    )(weight_grad, turned)
    return weight_grad, turned.T


def solution(mesh):
    return jax.shard_map(
        shards,
        mesh=mesh,
        in_specs=(P("crop", None), P("crop", None), P(None, "proto"), P(None, "proto")),
        out_specs=(P("crop", "proto"), P("crop", "proto")),
        check_vma=False,
    )
```

time: 107 us -> 93.2 us (0.87)
  Pallas kernels: 103 us -> 89.2 us
    pallas_call x1, Pallas kernels: 103 us -> 87.5 us  [shards(): pl.pallas_call(functools.partial(kernel, factor), out_shape=(jax.ShapeDty...]
    pallas_call x0 -> x1, Pallas kernels: none -> 1.68 us  [shards(): pl.pallas_call(hand_over, out_shape=(jax.ShapeDtypeStruct(weight_grad.sha...]
    unnamed x2 -> x8, local copies, waits for them, and re-layouts: 3.09 us -> 3.14 us
where the time goes in v2:
time: 93.2 us; the launch traced here: 93 us
  Pallas kernels  89.2 us (96%)
  local copies, waits for them, and re-layouts  3.14 us (3%)
    pallas_call x1, Pallas kernels, shards(): pl.pallas_call(functools.partial(kernel, factor), out_shape=(jax.ShapeDty...  87.5 us
    unnamed x8, local copies, waits for them, and re-layouts  3.14 us

profile of v2, /device:TPU:1, one launch (start us, length us, event | category | flops | bytes accessed | tf_op | source)
XLA Modules:
  0.0 93.0 jit_solution(3980089319677746378)
XLA Ops:
  0.6 0.0 copy-start.1
  0.6 0.9 copy-done.1
  1.6 0.0 copy-start.2
  1.6 0.9 copy-done.2
  2.5 87.5 %prototype_head.1 = (f32[8,8192]{1,0:T(8,128)S(1)}, f32[32,384]{1,0:T(8,128)S(1)}) custom-call(bf16[384,256]{1,0:T(8,128)(2,1)S(1)} %copy-done.1, bf16[384,256]{1,0:T(8,128)(2,1)S(1)} %copy-done.2, bf16[256,8192]{1,0:T(8,128)(2,1)} %tw_hbm.1, bf16[256,8192]{1,0:T(8,128)(2,1)} %sw_hbm.1), custom_call_target="tpu_custom_call" | custom-call | tf_op jit(solution)/shard_map/prototype_head/pallas_call | solution.py:469
  90.0 0.0 copy-start
  90.0 0.7 copy-done
  90.7 0.0 copy-start.3
  90.7 0.6 copy-done.3
  91.3 1.7 %hand_over.1 = (f32[8,8192]{1,0:T(8,128)}, f32[32,384]{1,0:T(8,128)}) custom-call(f32[8,8192]{1,0:T(8,128)} %copy-done, f32[32,384]{1,0:T(8,128)} %copy-done.3), custom_call_target="tpu_custom_call" | custom-call | tf_op jit(solution)/shard_map/hand_over/pallas_call | solution.py:487
Async XLA Ops:
  0.6 0.9 copy-start.1
  1.6 0.9 copy-start.2
  90.0 0.7 copy-start
  90.7 0.6 copy-start.3

commit v3 on v2

--- a/solution.py
+++ b/solution.py
@@ -34,9 +34,9 @@
     wout_ref, hout_ref,
     E, A, tw_raw, sw_raw, tw_bf, sw_bf, sw_t, sw_inv, t_bf, s_bf, s_t, s_raw, s_inv,
     u_wide, part, t_src, s_src, t_in, s_in,
-    c_src, c_in, r_src, r_in, flat_ref, v_ref,
+    y_own, y_src, y_in, c_src, c_in, r_src, r_in, flat_ref,
     L, G, ring_r, ring_l, g_sum, g_out, h_core, h_in,
-    load_sem, t_send, t_recv, t_fsend, t_frecv, s_send, s_recv, s_fsend, s_frecv,
+    load_sem, y_send, y_recv, t_send, t_recv, t_fsend, t_frecv, s_send, s_recv, s_fsend, s_frecv,
     c_send, c_recv, r_send, r_recv,
     rr_send, rr_recv, rl_send, rl_recv, a_send, a_recv, hc_send, hc_recv, h_send, h_recv,
 ):
@@ -77,6 +77,13 @@
     load_t = pltpu.make_async_copy(tw_hbm.at[:, pl.ds(col0, TILE_COLS)], tw_raw, load_sem.at[0])
     load_s = pltpu.make_async_copy(sw_hbm.at[:, pl.ds(col0, TILE_COLS)], sw_raw, load_sem.at[1])
     load_t.start()
+    loads = {}
+    for o in (2, 1, 3):
+        col = pl.multiple_of(((y + o) % NY) * TILE_COLS, TILE_COLS)
+        loads[o] = pltpu.make_async_copy(
+            tw_hbm.at[:, pl.ds(col, TILE_COLS)], L.at[(o - 1) * D:o * D, :], load_sem.at[1 + o]
+        )
+        loads[o].start()
     load_s.start()
 
     def block_rows(block):
@@ -135,68 +142,102 @@
             wait_bytes(dst.at[way - 1, 1 - c, piece], frecv.at[way - 1, piece])
         return (y + NY - way) % NY, dst[way - 1].reshape(ROWS, D)
 
+    def cols_start(r, half, sums):
+        c_src[r, half] = jnp.sum(sums, axis=0, keepdims=True)
+        for i, dz in enumerate(line):
+            remote(
+                c_src.at[r, half], c_in.at[r, half, i], c_send.at[r, half], c_recv.at[r, half], dev(0, dz, 0, 0)
+            ).start()
+
+    def cols_done(r, half):
+        wait_bytes(c_in.at[r, half], c_recv.at[r, half])
+        total = c_src[r, half]
+        for i in range(len(line)):
+            total = total + c_in[r, half, i]
+        return 1.0 / total
+
     gather_start(t_src, t_in, t_send, t_recv)
     load_t.wait()
     normalise(tw_raw, tw_bf, None)
 
-    def exp_block(block, first):
+    def teacher_exp(rows, weight, cols):
+        return jnp.exp2(jnp.dot(t_bf[rows, :], weight[:, cols], preferred_element_type=F32) * (LOG2E / TEACHER_TEMP))
+
+    def halves(one):
+        def step(half, carry):
+            one(pl.ds(pl.multiple_of(half * HALF, HALF), HALF))
+            return carry
+
+        lax.fori_loop(0, 2, step, 0)
+
+    def exp_block(block):
         rows = block_rows(block)
 
-        def one(q, carry):
-            cols = pl.ds(pl.multiple_of(q * HALF, HALF), HALF)
-            e = jnp.exp2(
-                jnp.dot(t_bf[rows, :], tw_bf[:, cols], preferred_element_type=F32) * (LOG2E / TEACHER_TEMP)
-            )
-            E[rows, cols] = e
+        def one(cols):
+            E[rows, cols] = teacher_exp(rows, tw_bf, cols)
+
+        halves(one)
+
+    def own_sums(weight, dst, keep):
+        rows = block_rows(y)
+
+        def one(cols):
+            e = teacher_exp(rows, weight, cols)
+            if keep:
+                E[rows, cols] = e
             sums = jnp.sum(e.reshape(ROWS // 8, 8, HALF), axis=0)
-            v_ref[:, cols] = sums if first else sums + v_ref[:, cols]
-            return carry
-
-        lax.fori_loop(0, 2, one, 0)
-
-    exp_block(y, True)
+            dst[:, cols] = jnp.sum(sums, axis=0, keepdims=True)
+
+        halves(one)
+
+    def sums_for(o):
+        loads[o].wait()
+        weight = L.at[(NY + o - 2) * D:(NY + o - 1) * D, :]
+        normalise(L.at[(o - 1) * D:o * D, :], weight, None)
+        own_sums(weight, y_src.at[o - 1], False)
+        remote(y_src.at[o - 1], y_in.at[o - 1], y_send, y_recv.at[o - 1], dev(o, 0, 0, 0)).start()
+
+    own_sums(tw_bf, y_own, True)
+    sums_for(2)
+    sums_for(1)
     gather_relay(t_in, t_send, t_recv)
-    load_s.wait()
-    normalise(sw_raw, sw_bf, sw_inv)
+    sums_for(3)
     gather_near(t_in, t_recv, t_fsend, t_frecv)
+    for o in range(1, NY):
+        wait_bytes(y_in.at[o - 1], y_recv.at[o - 1])
+    col_sums = y_own[...] + y_in[0] + y_in[1] + y_in[2]
+    cols_start(0, 0, col_sums[:, :HALF])
+    cols_start(0, 1, col_sums[:, HALF:])
     for way in (1, 3, 2):
         if way == 3:
             gather_far(t_in, t_recv, t_fsend, t_frecv)
         block, rows = gather_done(t_in, t_frecv, way)
         t_bf[block_rows(block), :] = rows.astype(BF16)
-        exp_block(block, False)
-
-    def cols_start(r, sums):
-        c_src[r] = jnp.sum(sums, axis=0, keepdims=True)
-        for i, dz in enumerate(line):
-            remote(c_src.at[r], c_in.at[r, i], c_send.at[r], c_recv.at[r], dev(0, dz, 0, 0)).start()
-
-    def cols_done(r):
-        wait_bytes(c_in.at[r], c_recv.at[r])
-        total = c_src[r]
-        for i in range(len(line)):
-            total = total + c_in[r, i]
-        return 1.0 / total
+        exp_block(block)
+    gather_start(s_src, s_in, s_send, s_recv)
 
     lane = lax.broadcasted_iota(jnp.int32, (8, 128), 1)
     sublane = lax.broadcasted_iota(jnp.int32, (8, 128), 0)
 
-    def rows_of(src, r, scale, store):
-        def one(b, carry):
-            rows = pl.ds(pl.multiple_of(b * 128, 128), 128)
-            acc = None
-            for k in range(TILE_COLS // 128):
-                cols = slice(k * 128, (k + 1) * 128)
-                term = src[rows, cols]
-                if scale is not None:
-                    term = term * scale[:, cols]
-                if store:
-                    src[rows, cols] = term
-                acc = term if acc is None else acc + term
-            part[rows, :] = acc
-            return carry
-
-        lax.fori_loop(0, BLOCKS, one, 0)
+    def rows_of(src, r, scaled, store):
+        for half in range(2):
+            scale = cols_done(r, half) if scaled else None
+
+            def one(b, carry):
+                rows = pl.ds(pl.multiple_of(b * 128, 128), 128)
+                acc = part[rows, :] if half else None
+                for k in range(HALF // 128):
+                    cols = slice(half * HALF + k * 128, half * HALF + (k + 1) * 128)
+                    term = src[rows, cols]
+                    if scaled:
+                        term = term * scale[:, k * 128:(k + 1) * 128]
+                    if store:
+                        src[rows, cols] = term
+                    acc = term if acc is None else acc + term
+                part[rows, :] = acc
+                return carry
+
+            lax.fori_loop(0, BLOCKS, one, 0)
 
         def packed(g0, g1):
             out = None
@@ -229,19 +270,20 @@
             value = low[:, g:g + 1] if g < 128 else high[:, g - 128:g - 127]
             dst[8 * g:8 * g + 8, :] = jnp.broadcast_to(value, (8, 128))
 
-    def cols_of():
-        def one(b, acc):
-            rows = pl.ds(pl.multiple_of(b * 128, 128), 128)
-            u = u_wide[rows, :]
-            out = []
-            for k in range(TILE_COLS // 128):
-                e = E[rows, k * 128:(k + 1) * 128] * u
-                out.append(acc[k] + jnp.sum(e.reshape(16, 8, 128), axis=0))
-            return tuple(out)
-
-        zero = tuple(jnp.zeros((8, 128), F32) for _ in range(TILE_COLS // 128))
-        acc = lax.fori_loop(0, BLOCKS, one, zero)
-        return jnp.concatenate(acc, axis=1)
+    def cols_of(r):
+        for half in range(2):
+
+            def one(b, acc):
+                rows = pl.ds(pl.multiple_of(b * 128, 128), 128)
+                u = u_wide[rows, :]
+                out = []
+                for k in range(HALF // 128):
+                    e = E[rows, half * HALF + k * 128:half * HALF + (k + 1) * 128] * u
+                    out.append(acc[k] + jnp.sum(e.reshape(16, 8, 128), axis=0))
+                return tuple(out)
+
+            zero = tuple(jnp.zeros((8, 128), F32) for _ in range(HALF // 128))
+            cols_start(r, half, jnp.concatenate(lax.fori_loop(0, BLOCKS, one, zero), axis=1))
 
     def student_exp():
         def one(i, carry):
@@ -262,31 +304,28 @@
         s_inv[rows, :] = jnp.broadcast_to(inv, (ROWS, 128))
         s_bf[rows, :] = unit.astype(BF16)
 
-    cols_start(0, v_ref[...])
-    gather_start(s_src, s_in, s_send, s_recv)
-    student_block(y, s_src[...].reshape(ROWS, D))
+    rows_of(E, 0, True, False)
+    rows_start(0)
+    load_s.wait()
+    normalise(sw_raw, sw_bf, sw_inv)
     for q in range(4):
         sw_t[q * QUARTER:(q + 1) * QUARTER, :] = sw_bf[:, q * QUARTER:(q + 1) * QUARTER].T
-    v = cols_done(0)
-    rows_of(E, 0, v, False)
-    rows_start(0)
+    student_block(y, s_src[...].reshape(ROWS, D))
     gather_relay(s_in, s_send, s_recv)
+    rows_done(0, u_wide, 1.0)
+    cols_of(1)
     gather_near(s_in, s_recv, s_fsend, s_frecv)
-    rows_done(0, u_wide, 1.0)
-    cols_start(1, cols_of())
     gather_far(s_in, s_recv, s_fsend, s_frecv)
     for way in (1, 3, 2):
         student_block(*gather_done(s_in, s_frecv, way))
-    v = cols_done(1)
-    rows_of(E, 1, v, False)
+    rows_of(E, 1, True, False)
     rows_start(1)
     student_exp()
     rows_done(1, u_wide, 1.0)
-    cols_start(2, cols_of())
-    rows_of(A, 3, None, False)
+    cols_of(2)
+    rows_of(A, 3, False, False)
     rows_start(3)
-    v = cols_done(2)
-    rows_of(E, 2, v, True)
+    rows_of(E, 2, True, True)
     rows_start(2)
     for b in range(BLOCKS):
         s_t[:, b * 128:(b + 1) * 128] = s_bf[b * 128:(b + 1) * 128, :].T
@@ -419,8 +458,10 @@
     for buf, send, fsend in ((t_in, t_send, t_fsend), (s_in, s_send, s_fsend)):
         wait_bytes(buf.at[:, 0], send)
         wait_bytes(buf.at[:, 0], fsend)
+    wait_bytes(y_in, y_send)
     for r in range(BALANCE_STEPS):
-        wait_bytes(c_in.at[r], c_send.at[r])
+        for half in range(2):
+            wait_bytes(c_in.at[r, half], c_send.at[r, half])
     for r in range(BALANCE_STEPS + 1):
         wait_bytes(r_in.at[r], r_send.at[r])
     for q in range(4):
@@ -451,18 +492,19 @@
         v((TILE_ROWS, 128), F32), v((TILE_ROWS, 128), F32),
         v((2, 2, PIECE, D), F32), v((2, 2, PIECE, D), F32),
         v((NY - 1, 2, 2, PIECE, D), F32), v((NY - 1, 2, 2, PIECE, D), F32),
-        v((BALANCE_STEPS, 1, TILE_COLS), F32), v((BALANCE_STEPS, NZ - 1, 1, TILE_COLS), F32),
+        v((1, TILE_COLS), F32), v((NY - 1, 1, TILE_COLS), F32), v((NY - 1, 1, TILE_COLS), F32),
+        v((BALANCE_STEPS, 2, 1, HALF), F32), v((BALANCE_STEPS, 2, NZ - 1, 1, HALF), F32),
         v((BALANCE_STEPS + 1, BLOCKS, 128), F32), v((BALANCE_STEPS + 1, peers, BLOCKS, 128), F32),
-        v((16, 128), F32), v((8, TILE_COLS), F32),
+        v((16, 128), F32),
         v((TILE_ROWS, TILE_COLS), BF16),
         v((4, NY, NZ, 8, QUARTER), F32),
         v((4, NZ // 2, NY, 8, QUARTER), F32), v((4, NZ // 2, NY, 8, QUARTER), F32),
         v((4, NY, 8, QUARTER), F32), v((4, NY - 1, 8, QUARTER), F32),
         v((NX * 32, TILE_ROWS), F32), v((sheet, 32, ROWS), F32),
-        dma((2,)),
+        dma((5,)), dma, dma((3,)),
         dma, dma((3, 2)), dma, dma((3, 2)),
         dma, dma((3, 2)), dma, dma((3, 2)),
-        dma((3,)), dma((3,)), dma((4,)), dma((4,)),
+        dma((3, 2)), dma((3, 2)), dma((4,)), dma((4,)),
         dma((4, 4)), dma((4, 4)), dma((4, 4)), dma((4, 4)),
         dma((4,)), dma((4,)), dma, dma, dma, dma,
     ]
@@ -480,20 +522,6 @@
         ),
         name="prototype_head",
     )(teacher_features, student_features, teacher_weight, student_weight)
-    def hand_over(a_ref, b_ref, a_out, b_out):
-        a_out[...] = a_ref[...]
-        b_out[...] = b_ref[...]
-
-    weight_grad, turned = pl.pallas_call(
-        hand_over,
-        out_shape=(
-            jax.ShapeDtypeStruct(weight_grad.shape, F32),
-            jax.ShapeDtypeStruct(turned.shape, F32),
-        ),
-        in_specs=[vmem, vmem],
-        out_specs=(vmem, vmem),
-        name="hand_over",
-    )(weight_grad, turned)
     return weight_grad, turned.T
 
 

time: 93.2 us -> 89.4 us (0.959)
  Pallas kernels: 89.2 us -> 85.5 us
    pallas_call x1, Pallas kernels: 87.5 us -> 85.5 us  [shards(): pl.pallas_call(functools.partial(kernel, factor), out_shape=(jax.ShapeDty...]
    pallas_call x1 -> x0, Pallas kernels: 1.68 us -> none  [shards(): pl.pallas_call(hand_over, out_shape=(jax.ShapeDtypeStruct(weight_grad.sha...]
    unnamed x8 -> x6, local copies, waits for them, and re-layouts: 3.14 us -> 3.17 us
where the time goes in v3:
time: 89.4 us; the launch traced here: 89.3 us
  Pallas kernels  85.5 us (96%)
  local copies, waits for them, and re-layouts  3.17 us (4%)
    pallas_call x1, Pallas kernels, shards(): pl.pallas_call(functools.partial(kernel, factor), out_shape=(jax.ShapeDty...  85.5 us
    unnamed x6, local copies, waits for them, and re-layouts  3.17 us

profile of v3, /device:TPU:1, one launch (start us, length us, event | category | flops | bytes accessed | tf_op | source)
XLA Modules:
  0.0 89.3 jit_solution(15858815110921967528)
XLA Ops:
  0.6 0.0 copy-start
  0.6 0.9 %copy-done = bf16[384,256]{1,0:T(8,128)(2,1)S(1)} copy-done((bf16[384,256]{1,0:T(8,128)(2,1)S(1)}, bf16[384,256]{1,0:T(8,128)(2,1)}, u32[]{:S(2)}) %copy-start) | copy-done | bytes 196632
  1.6 0.0 copy-start.1
  1.6 0.9 %copy-done.1 = bf16[384,256]{1,0:T(8,128)(2,1)S(1)} copy-done((bf16[384,256]{1,0:T(8,128)(2,1)S(1)}, bf16[384,256]{1,0:T(8,128)(2,1)}, u32[]{:S(2)}) %copy-start.1) | copy-done | bytes 196632
  2.5 85.5 %prototype_head.1 = (f32[8,8192]{1,0:T(8,128)S(1)}, f32[32,384]{1,0:T(8,128)S(1)}) custom-call(bf16[384,256]{1,0:T(8,128)(2,1)S(1)} %copy-done, bf16[384,256]{1,0:T(8,128)(2,1)S(1)} %copy-done.1, bf16[256,8192]{1,0:T(8,128)(2,1)} %tw_hbm.1, bf16[256,8192]{1,0:T(8,128)(2,1)} %sw_hbm.1), custom_call_target="tpu_custom_call" | custom-call | tf_op jit(solution)/shard_map/prototype_head/pallas_call | solution.py:511
  88.0 0.7 copy.8
  88.7 0.6 copy.9
Async XLA Ops:
  0.6 0.9 %copy-start = (bf16[384,256]{1,0:T(8,128)(2,1)S(1)}, bf16[384,256]{1,0:T(8,128)(2,1)}, u32[]{:S(2)}) copy-start(bf16[384,256]{1,0:T(8,128)(2,1)} %t_ref.1) | copy-start | bytes 589828
  1.6 0.9 %copy-start.1 = (bf16[384,256]{1,0:T(8,128)(2,1)S(1)}, bf16[384,256]{1,0:T(8,128)(2,1)}, u32[]{:S(2)}) copy-start(bf16[384,256]{1,0:T(8,128)(2,1)} %s_ref.1) | copy-start | bytes 589828

commit v4 on v3

--- a/solution.py
+++ b/solution.py
@@ -200,8 +200,8 @@
     own_sums(tw_bf, y_own, True)
     sums_for(2)
     sums_for(1)
+    sums_for(3)
     gather_relay(t_in, t_send, t_recv)
-    sums_for(3)
     gather_near(t_in, t_recv, t_fsend, t_frecv)
     for o in range(1, NY):
         wait_bytes(y_in.at[o - 1], y_recv.at[o - 1])
@@ -479,6 +479,7 @@
     factor = LOSS_SCALE / (STUDENT_TEMP * crops_all)
     vmem = pl.BlockSpec(memory_space=pltpu.VMEM)
     hbm = pl.BlockSpec(memory_space=pl.ANY)
+    far_memory = pl.BlockSpec(memory_space=pltpu.HBM)
     peers, sheet = NY * NX * NC - 1, NY * NX - 1
     v = pltpu.VMEM
     dma = pltpu.SemaphoreType.DMA
@@ -522,6 +523,28 @@
         ),
         name="prototype_head",
     )(teacher_features, student_features, teacher_weight, student_weight)
+    def hand_over(a_ref, b_ref, a_out, b_out, sem):
+        copies = [
+            pltpu.make_async_copy(a_ref, a_out, sem.at[0]),
+            pltpu.make_async_copy(b_ref, b_out, sem.at[1]),
+        ]
+        for copy in copies:
+            copy.start()
+        for copy in copies:
+            copy.wait()
+
+    weight_grad, turned = pl.pallas_call(
+        hand_over,
+        out_shape=(
+            jax.ShapeDtypeStruct(weight_grad.shape, F32),
+            jax.ShapeDtypeStruct(turned.shape, F32),
+        ),
+        in_specs=[vmem, vmem],
+        out_specs=(far_memory, far_memory),
+        scratch_shapes=[dma((2,))],
+        compiler_params=pltpu.CompilerParams(vmem_limit_bytes=2 * 1024 * 1024),
+        name="hand_over",
+    )(weight_grad, turned)
     return weight_grad, turned.T
 
 

time: 89.4 us -> 88.6 us (level)
  local copies, waits for them, and re-layouts: 3.17 us -> 1.85 us
    unnamed x6 -> x4, local copies, waits for them, and re-layouts: 3.17 us -> 1.85 us
where the time goes in v4:
time: 88.6 us; the launch traced here: 88.5 us
  Pallas kernels  86 us (97%)
  local copies, waits for them, and re-layouts  1.85 us (2%)
    pallas_call x1, Pallas kernels, shards(): pl.pallas_call(functools.partial(kernel, factor), out_shape=(jax.ShapeDty...  85.3 us
    unnamed x4, local copies, waits for them, and re-layouts  1.85 us

profile of v4, /device:TPU:1, one launch (start us, length us, event | category | flops | bytes accessed | tf_op | source)
XLA Modules:
  0.0 88.5 jit_solution(14377189345027338635)
XLA Ops:
  0.6 0.0 copy-start
  0.6 0.9 %copy-done = bf16[384,256]{1,0:T(8,128)(2,1)S(1)} copy-done((bf16[384,256]{1,0:T(8,128)(2,1)S(1)}, bf16[384,256]{1,0:T(8,128)(2,1)}, u32[]{:S(2)}) %copy-start) | copy-done | bytes 196632
  1.6 0.0 copy-start.1
  1.6 0.9 %copy-done.1 = bf16[384,256]{1,0:T(8,128)(2,1)S(1)} copy-done((bf16[384,256]{1,0:T(8,128)(2,1)S(1)}, bf16[384,256]{1,0:T(8,128)(2,1)}, u32[]{:S(2)}) %copy-start.1) | copy-done | bytes 196632
  2.5 85.3 %prototype_head.1 = (f32[8,8192]{1,0:T(8,128)S(1)}, f32[32,384]{1,0:T(8,128)S(1)}) custom-call(bf16[384,256]{1,0:T(8,128)(2,1)S(1)} %copy-done, bf16[384,256]{1,0:T(8,128)(2,1)S(1)} %copy-done.1, bf16[256,8192]{1,0:T(8,128)(2,1)} %tw_hbm.1, bf16[256,8192]{1,0:T(8,128)(2,1)} %sw_hbm.1), custom_call_target="tpu_custom_call" | custom-call | tf_op jit(solution)/shard_map/prototype_head/pallas_call | solution.py:512
  87.8 0.7 hand_over.1
Async XLA Ops:
  0.6 0.9 %copy-start = (bf16[384,256]{1,0:T(8,128)(2,1)S(1)}, bf16[384,256]{1,0:T(8,128)(2,1)}, u32[]{:S(2)}) copy-start(bf16[384,256]{1,0:T(8,128)(2,1)} %t_ref.1) | copy-start | bytes 589828
  1.6 0.9 %copy-start.1 = (bf16[384,256]{1,0:T(8,128)(2,1)S(1)}, bf16[384,256]{1,0:T(8,128)(2,1)}, u32[]{:S(2)}) copy-start(bf16[384,256]{1,0:T(8,128)(2,1)} %s_ref.1) | copy-start | bytes 589828

commit v5 on v4

--- a/solution.py
+++ b/solution.py
@@ -76,7 +76,6 @@
     col0 = pl.multiple_of(y * TILE_COLS, TILE_COLS)
     load_t = pltpu.make_async_copy(tw_hbm.at[:, pl.ds(col0, TILE_COLS)], tw_raw, load_sem.at[0])
     load_s = pltpu.make_async_copy(sw_hbm.at[:, pl.ds(col0, TILE_COLS)], sw_raw, load_sem.at[1])
-    load_t.start()
     loads = {}
     for o in (2, 1, 3):
         col = pl.multiple_of(((y + o) % NY) * TILE_COLS, TILE_COLS)
@@ -84,6 +83,7 @@
             tw_hbm.at[:, pl.ds(col, TILE_COLS)], L.at[(o - 1) * D:o * D, :], load_sem.at[1 + o]
         )
         loads[o].start()
+    load_t.start()
     load_s.start()
 
     def block_rows(block):
@@ -157,8 +157,6 @@
         return 1.0 / total
 
     gather_start(t_src, t_in, t_send, t_recv)
-    load_t.wait()
-    normalise(tw_raw, tw_bf, None)
 
     def teacher_exp(rows, weight, cols):
         return jnp.exp2(jnp.dot(t_bf[rows, :], weight[:, cols], preferred_element_type=F32) * (LOG2E / TEACHER_TEMP))
@@ -197,10 +195,12 @@
         own_sums(weight, y_src.at[o - 1], False)
         remote(y_src.at[o - 1], y_in.at[o - 1], y_send, y_recv.at[o - 1], dev(o, 0, 0, 0)).start()
 
-    own_sums(tw_bf, y_own, True)
     sums_for(2)
     sums_for(1)
     sums_for(3)
+    load_t.wait()
+    normalise(tw_raw, tw_bf, None)
+    own_sums(tw_bf, y_own, True)
     gather_relay(t_in, t_send, t_recv)
     gather_near(t_in, t_recv, t_fsend, t_frecv)
     for o in range(1, NY):

time: 88.6 us -> 88.3 us (level)
  no operation moved by 1% of the time
where the time goes in v5:
time: 88.3 us; the launch traced here: 88.2 us
  Pallas kernels  85.7 us (97%)
  local copies, waits for them, and re-layouts  1.85 us (2%)
    pallas_call x1, Pallas kernels, shards(): pl.pallas_call(functools.partial(kernel, factor), out_shape=(jax.ShapeDty...  85 us
    unnamed x4, local copies, waits for them, and re-layouts  1.85 us

profile of v5, /device:TPU:1, one launch (start us, length us, event | category | flops | bytes accessed | tf_op | source)
XLA Modules:
  0.0 88.2 jit_solution(14906589902159188212)
XLA Ops:
  0.6 0.0 copy-start
  0.6 0.9 %copy-done = bf16[384,256]{1,0:T(8,128)(2,1)S(1)} copy-done((bf16[384,256]{1,0:T(8,128)(2,1)S(1)}, bf16[384,256]{1,0:T(8,128)(2,1)}, u32[]{:S(2)}) %copy-start) | copy-done | bytes 196632
  1.6 0.0 copy-start.1
  1.6 0.9 %copy-done.1 = bf16[384,256]{1,0:T(8,128)(2,1)S(1)} copy-done((bf16[384,256]{1,0:T(8,128)(2,1)S(1)}, bf16[384,256]{1,0:T(8,128)(2,1)}, u32[]{:S(2)}) %copy-start.1) | copy-done | bytes 196632
  2.5 85.0 %prototype_head.1 = (f32[8,8192]{1,0:T(8,128)S(1)}, f32[32,384]{1,0:T(8,128)S(1)}) custom-call(bf16[384,256]{1,0:T(8,128)(2,1)S(1)} %copy-done, bf16[384,256]{1,0:T(8,128)(2,1)S(1)} %copy-done.1, bf16[256,8192]{1,0:T(8,128)(2,1)} %tw_hbm.1, bf16[256,8192]{1,0:T(8,128)(2,1)} %sw_hbm.1), custom_call_target="tpu_custom_call" | custom-call | tf_op jit(solution)/shard_map/prototype_head/pallas_call | solution.py:512
  87.5 0.7 hand_over.1
Async XLA Ops:
  0.6 0.9 %copy-start = (bf16[384,256]{1,0:T(8,128)(2,1)S(1)}, bf16[384,256]{1,0:T(8,128)(2,1)}, u32[]{:S(2)}) copy-start(bf16[384,256]{1,0:T(8,128)(2,1)} %t_ref.1) | copy-start | bytes 589828
  1.6 0.9 %copy-start.1 = (bf16[384,256]{1,0:T(8,128)(2,1)S(1)}, bf16[384,256]{1,0:T(8,128)(2,1)}, u32[]{:S(2)}) copy-start(bf16[384,256]{1,0:T(8,128)(2,1)} %s_ref.1) | copy-start | bytes 589828
